TPU v7x, 256 devices: a whole 4x4x8 slice. The times are simulated.
256 devices in a mesh: group: 16 (over z, core), local: 16 (over y, x).
Axes of the slice: x: 4, y: 4, z: 8, core: 2. Of those that a mesh axis runs over, the one named last changes fastest.
Arguments:
- tokens: bfloat16 [16384, 4096], P(('group', 'local')), may hold values from -6 to 6
- segment_ids: int32 [16384, 12], P(('group', 'local')), may hold values from 0 to 255, as said below
- segment_count: int32 [16384], P(('group', 'local')), may hold values from 4 to 12
- gate_values: bfloat16 [16384, 12], P(('group', 'local')), may hold values from 0.099609375 to 1
- gate_weight: bfloat16 [256, 4096, 384], P(('group', 'local')), may hold values from -0.09375 to 0.09375
- up_weight: bfloat16 [256, 4096, 384], P(('group', 'local')), may hold values from -0.09375 to 0.09375
- down_weight: bfloat16 [256, 384, 4096], P(('group', 'local')), may hold values from -0.3125 to 0.3125
Outputs:
- mixed: bfloat16 [16384, 4096], P(('group', 'local'))
Inputs may be any that keep to these rules, and one draw needn't show every extreme that they name: `segment_ids`: segment s is held by device s of the mesh and lies in group s // 16. A token's first segment_count entries are distinct and lie in exactly 4 groups with consecutive numbers modulo 16, one to three segments a group with consecutive local numbers modulo 16, listed group by group; later entries are not used. Of one device's tokens exactly 16 name segments of each group, and at most 3 name any one segment.
All inputs are finite; a program needn't handle non-finite values.
Results may differ from a plain program's by a relative error of at most 0.0064.
Values may be sent and summed in bfloat16 or wider, within the bound.
A program may use at most 128 MiB of HBM per device.

v0:
```python
import jax
import jax.numpy as jnp
from jax import lax
from jax.sharding import PartitionSpec as P

GROUPS_TOK = 4


def slot_table(present, capacity, axis):
    counted = present.astype(jnp.int32)
    before = jnp.cumsum(counted, axis=axis) - counted
    places = lax.broadcasted_iota(jnp.int32, before.shape + (capacity,), before.ndim)
    return present[..., None] & (before[..., None] == places)


def weighted_terms(gathered, weights, gate_block, up_block, down_block):
    shape_in = gathered.shape
    flat_rows = gathered.reshape(-1, shape_in[-1])
    gated = jnp.dot(flat_rows, gate_block, preferred_element_type=jnp.float32)
    upward = jnp.dot(flat_rows, up_block, preferred_element_type=jnp.float32)
    hidden = (jax.nn.silu(gated) * upward).astype(jnp.bfloat16)
    output = jnp.dot(hidden, down_block, preferred_element_type=jnp.float32)
    scaled = weights.reshape(-1, 1).astype(jnp.float32) * output
    return scaled.astype(jnp.bfloat16).reshape(shape_in)


def on_device(tokens, segment_ids, segment_count, gate_values, gate_weight, up_weight, down_weight):
    group_count = lax.axis_size("group")
    local_count = lax.axis_size("local")
    token_count, slot_width = segment_ids.shape
    model_width = tokens.shape[1]
    segments = group_count * local_count
    group_slots = GROUPS_TOK * token_count // group_count
    owner_slots = 3 * group_slots // local_count
    is_valid = (
        lax.broadcasted_iota(jnp.int32, (token_count, slot_width), 1) < segment_count[:, None]
    )
    labels = lax.broadcasted_iota(jnp.int32, (1, 1, segments), 2)
    hits = is_valid[:, :, None] & (segment_ids[:, :, None] == labels)
    seg_gate = jnp.sum(jnp.where(hits, gate_values.astype(jnp.float32)[:, :, None], 0.0), axis=1)
    gate_block = gate_weight[0]
    up_block = up_weight[0]
    down_block = down_weight[0]
    token_index = lax.broadcasted_iota(jnp.int32, (token_count, 1, 1), 0)
    match = slot_table(seg_gate > 0, owner_slots, 0)
    source = jnp.sum(match.astype(jnp.int32) * token_index, axis=0)
    filled = jnp.any(match, axis=0)
    slot_gate = jnp.sum(jnp.where(match, seg_gate[:, :, None], 0.0), axis=0).astype(jnp.bfloat16)
    sending = jnp.where(filled[:, :, None], tokens[source], jnp.zeros((), jnp.bfloat16))
    sending = sending.reshape(group_count, local_count, owner_slots, model_width)
    slot_gate = slot_gate.reshape(group_count, local_count, owner_slots)
    recv_rows, recv_gate = (
        lax.all_to_all(
            lax.all_to_all(sending, "group", split_axis=0, concat_axis=0, tiled=True),
            "local",
            split_axis=1,
            concat_axis=1,
            tiled=True,
        ),
        lax.all_to_all(
            lax.all_to_all(slot_gate, "group", split_axis=0, concat_axis=0, tiled=True),
            "local",
            split_axis=1,
            concat_axis=1,
            tiled=True,
        ),
    )
    terms = weighted_terms(recv_rows, recv_gate, gate_block, up_block, down_block)
    returned = lax.all_to_all(
        lax.all_to_all(terms, "group", split_axis=0, concat_axis=0, tiled=True),
        "local",
        split_axis=1,
        concat_axis=1,
        tiled=True,
    )
    selector = match.astype(jnp.bfloat16).reshape(
        token_count, group_count, local_count * owner_slots
    )
    returned = returned.reshape(group_count, local_count * owner_slots, model_width)
    parts = jnp.einsum("tgk,gkd->gtd", selector, returned, preferred_element_type=jnp.float32)
    rounded = lax.optimization_barrier(parts.astype(jnp.bfloat16))
    return jnp.sum(rounded.astype(jnp.float32), axis=0).astype(jnp.bfloat16)


def solution(mesh):
    return jax.shard_map(
        on_device,
        mesh=mesh,
        in_specs=(
            P(("group", "local"), None),
            P(("group", "local"), None),
            P(("group", "local")),
            P(("group", "local"), None),
            P(("group", "local"), None, None),
            P(("group", "local"), None, None),
            P(("group", "local"), None, None),
        ),
        out_specs=P(("group", "local"), None),
        check_vma=False,
    )
```

profile of v0, /device:TPU:1, one launch (start us, length us, event | category | flops | bytes accessed | tf_op | source)
XLA Modules:
  0.0 668.0 jit_solution(6536850909687875705)
XLA Ops:
  0.0 0.0 copy-start
  0.0 0.8 convert_element_type.45
  0.8 0.8 iota_compare_fusion.2
  1.6 1.1 select_reduce_fusion
  2.7 0.1 copy.77
  2.8 0.7 copy.75
  3.5 0.1 reduce_window_sum.11
  3.6 0.1 copy.76
  3.7 1.9 select_reduce_fusion.2
  5.6 1.6 copy.79
  7.2 10.0 %all-to-all-start = ((bf16[16,16,3]{1,2,0:T(4,128)(2,1)}), bf16[16,16,3]{1,2,0:T(4,128)(2,1)}, u32[]{:S(2)}, u32[]{:S(2)}) async-start(bf16[16,16,3]{1,2,0:T(4,128)(2,1)} %copy.79), calls=%async_computation | async-start | bytes 32768 | tf_op jit(solution)/shard_map/all_to_all | solution.py:61
  17.2 4.4 select_reduce_fusion.1
  21.6 0.2 reshape.89
  21.8 13.1 %gather_fusion = bf16[768,4096]{1,0:T(8,128)(2,1)} fusion(bf16[64,4096]{1,0:T(8,128)(2,1)} %param.7, s32[1024]{0:T(1024)S(1)} %pad_clamp_fusion), kind=kCustom, calls=%fused_computation | custom fusion | bytes 12585984 | tf_op jit(solution)/shard_map/gather | solution.py:49
  34.9 12.9 %gather.6 = bf16[16,16,3,4096]{3,2,1,0:T(4,128)(2,1)} reshape(bf16[768,4096]{1,0:T(8,128)(2,1)} %gather_fusion) | data formatting | bytes 12582912 | tf_op jit(solution)/shard_map/gather | solution.py:49
  47.8 4.4 reduce_or.9
  52.3 6.2 broadcast_select_fusion
  58.5 7.7 %copy.83 = bf16[16,16,3,4096]{3,1,2,0:T(8,128)(2,1)} copy(bf16[16,16,3,4096]{3,2,1,0:T(4,128)(2,1)S(1)} %broadcast_select_fusion) | data formatting | bytes 12582912 | tf_op jit(solution)/shard_map/jit(_where)/select_n | solution.py:49
  66.2 0.0 all-to-all-done
  66.2 7.2 %all-to-all-start.2 = ((bf16[16,16,3,4096]{3,1,2,0:T(8,128)(2,1)}), bf16[16,16,3,4096]{3,1,2,0:T(8,128)(2,1)}, u32[]{:S(2)}, u32[]{:S(2)}) async-start(bf16[16,16,3,4096]{3,1,2,0:T(8,128)(2,1)} %copy.83), calls=%async_computation.2 | async-start | bytes 12582912 | tf_op jit(solution)/shard_map/all_to_all | solution.py:54
  73.4 1.4 copy.80
  74.8 137.1 %all-to-all-done.2 = bf16[16,16,3,4096]{3,1,2,0:T(8,128)(2,1)} async-done(((bf16[16,16,3,4096]{3,1,2,0:T(8,128)(2,1)}), bf16[16,16,3,4096]{3,1,2,0:T(8,128)(2,1)}, u32[]{:S(2)}, u32[]{:S(2)}) %all-to-all-start.2) | async-done | bytes 6291488 | tf_op jit(solution)/shard_map/all_to_all | solution.py:54
  212.0 6.8 %all-to-all-start.1 = ((bf16[16,16,3]{0,2,1:T(4,128)(2,1)}), bf16[16,16,3]{0,2,1:T(4,128)(2,1)S(1)}, u32[]{:S(2)}, u32[]{:S(2)}) async-start(bf16[16,16,3]{0,2,1:T(4,128)(2,1)} %copy.80), calls=%async_computation.1 | async-start | bytes 32768 | tf_op jit(solution)/shard_map/all_to_all | solution.py:60
  218.7 8.8 %copy.84 = bf16[16,16,3,4096]{3,0,2,1:T(8,128)(2,1)} copy(bf16[16,16,3,4096]{3,1,2,0:T(8,128)(2,1)} %all-to-all-done.2) | data formatting | bytes 12582912 | tf_op jit(solution)/shard_map/all_to_all | solution.py:54
  227.5 0.0 all-to-all-done.1
  227.5 6.9 %all-to-all-start.3 = ((bf16[16,16,3,4096]{3,0,2,1:T(8,128)(2,1)}), bf16[16,16,3,4096]{3,0,2,1:T(8,128)(2,1)}, u32[]{:S(2)}, u32[]{:S(2)}) async-start(bf16[16,16,3,4096]{3,0,2,1:T(8,128)(2,1)} %copy.84), calls=%async_computation.3 | async-start | bytes 12582912 | tf_op jit(solution)/shard_map/all_to_all | solution.py:53
  234.5 0.1 copy.81
  234.6 0.2 copy.82
  234.7 0.2 reshape.86
  234.9 91.0 %all-to-all-done.3 = bf16[16,16,3,4096]{3,0,2,1:T(8,128)(2,1)} async-done(((bf16[16,16,3,4096]{3,0,2,1:T(8,128)(2,1)}), bf16[16,16,3,4096]{3,0,2,1:T(8,128)(2,1)}, u32[]{:S(2)}, u32[]{:S(2)}) %all-to-all-start.3) | async-done | bytes 6291488 | tf_op jit(solution)/shard_map/all_to_all | solution.py:53
  325.9 11.4 %copy.85 = bf16[16,16,3,4096]{3,2,1,0:T(4,128)(2,1)} copy(bf16[16,16,3,4096]{3,0,2,1:T(8,128)(2,1)} %all-to-all-done.3) | data formatting | bytes 12582912 | tf_op jit(solution)/shard_map/all_to_all | solution.py:53
  337.3 13.7 %reshape.83 = bf16[768,4096]{1,0:T(8,128)(2,1)} reshape(bf16[16,16,3,4096]{3,2,1,0:T(4,128)(2,1)} %copy.85) | data formatting | bytes 12582912 | tf_op jit(solution)/shard_map/reshape | solution.py:18
  351.1 0.0 copy-start.1
  351.1 0.0 copy-start.2
  351.1 6.6 fusion.4
  357.7 0.0 copy-done.1
  357.7 0.0 copy-done.2
  357.7 3.5 fusion.9
  361.2 0.0 copy-done
  361.2 5.3 multiply_convert_fusion
  366.5 13.3 %reshape.84 = bf16[16,16,3,4096]{3,2,1,0:T(4,128)(2,1)} reshape(bf16[768,4096]{1,0:T(8,128)(2,1)} %multiply_convert_fusion) | data formatting | bytes 12582912 | tf_op jit(solution)/shard_map/reshape | solution.py:24
  379.8 8.5 %copy.86 = bf16[16,16,3,4096]{3,1,2,0:T(8,128)(2,1)S(1)} copy(bf16[16,16,3,4096]{3,2,1,0:T(4,128)(2,1)} %reshape.84) | data formatting | bytes 12582912 | tf_op jit(solution)/shard_map/reshape | solution.py:24
  388.2 148.6 %all_to_all.30 = bf16[16,16,3,4096]{3,1,2,0:T(8,128)(2,1)} all-to-all(bf16[16,16,3,4096]{3,1,2,0:T(8,128)(2,1)S(1)} %copy.86), channel_id=1, replica_groups=mesh['group'=16,'local'=16] {'group'}, dimensions={0} | all-to-all | bytes 12582912 | tf_op jit(solution)/shard_map/all_to_all | solution.py:70
  536.8 8.9 %copy.87 = bf16[16,16,3,4096]{3,0,2,1:T(8,128)(2,1)} copy(bf16[16,16,3,4096]{3,1,2,0:T(8,128)(2,1)} %all_to_all.30) | data formatting | bytes 12582912 | tf_op jit(solution)/shard_map/all_to_all | solution.py:70
  545.7 5.3 all-to-all-start.5
  551.1 0.9 eq.29
  551.9 1.2 eq.30
  553.2 1.5 and.23
  554.7 1.7 and.24
  556.4 0.1 iota.32
  556.5 90.6 %all-to-all-done.5 = bf16[16,16,3,4096]{3,0,2,1:T(8,128)(2,1)} async-done(((bf16[16,16,3,4096]{3,0,2,1:T(8,128)(2,1)}), bf16[16,16,3,4096]{3,0,2,1:T(8,128)(2,1)}, u32[]{:S(2)}, u32[]{:S(2)}) %all-to-all-start.5) | async-done | bytes 6291488 | tf_op jit(solution)/shard_map/all_to_all | solution.py:69
  647.1 14.9 %convolution_convert_fusion = bf16[16,64,4096]{2,1,0:T(8,128)(2,1)} fusion(bf16[16,48,4096]{2,0,1:T(8,128)(2,1)} %bitcast.5, pred[64,16,48]{0,2,1:T(8,128)(4,1)} %and.24, s32[64,16,48]{0,2,1:T(8,128)S(1)} %eq.30, s32[48]{0:T(128)S(1)} %iota.32), kind=kOutput, calls=%fused_computation.3 | convolution fusion | flops 406945792 | bytes 14926016 | tf_op jit(solution)/shard_map/tgk,gkd->gtd/dot_general | solution.py:80
  662.0 5.9 reduce_sum.45
  (5 shorter events, 0.0 us)
Async XLA Ops:
  0.0 361.2 %copy-start = (bf16[1,384,4096]{2,1,0:T(8,128)(2,1)S(1)}, bf16[1,384,4096]{2,1,0:T(8,128)(2,1)}, u32[]{:S(2)}) copy-start(bf16[1,384,4096]{2,1,0:T(8,128)(2,1)} %param.13) | copy-start | bytes 9437188
  7.2 59.0 %all-to-all-start = ((bf16[16,16,3]{1,2,0:T(4,128)(2,1)}), bf16[16,16,3]{1,2,0:T(4,128)(2,1)}, u32[]{:S(2)}, u32[]{:S(2)}) async-start(bf16[16,16,3]{1,2,0:T(4,128)(2,1)} %copy.79), calls=%async_computation | async-start | bytes 32768 | tf_op jit(solution)/shard_map/all_to_all | solution.py:61
  66.2 145.8 %all-to-all-start.2 = ((bf16[16,16,3,4096]{3,1,2,0:T(8,128)(2,1)}), bf16[16,16,3,4096]{3,1,2,0:T(8,128)(2,1)}, u32[]{:S(2)}, u32[]{:S(2)}) async-start(bf16[16,16,3,4096]{3,1,2,0:T(8,128)(2,1)} %copy.83), calls=%async_computation.2 | async-start | bytes 12582912 | tf_op jit(solution)/shard_map/all_to_all | solution.py:54
  212.0 15.6 %all-to-all-start.1 = ((bf16[16,16,3]{0,2,1:T(4,128)(2,1)}), bf16[16,16,3]{0,2,1:T(4,128)(2,1)S(1)}, u32[]{:S(2)}, u32[]{:S(2)}) async-start(bf16[16,16,3]{0,2,1:T(4,128)(2,1)} %copy.80), calls=%async_computation.1 | async-start | bytes 32768 | tf_op jit(solution)/shard_map/all_to_all | solution.py:60
  227.5 98.4 %all-to-all-start.3 = ((bf16[16,16,3,4096]{3,0,2,1:T(8,128)(2,1)}), bf16[16,16,3,4096]{3,0,2,1:T(8,128)(2,1)}, u32[]{:S(2)}, u32[]{:S(2)}) async-start(bf16[16,16,3,4096]{3,0,2,1:T(8,128)(2,1)} %copy.84), calls=%async_computation.3 | async-start | bytes 12582912 | tf_op jit(solution)/shard_map/all_to_all | solution.py:53
  351.1 6.6 copy-start.1
  351.1 6.6 copy-start.2
  545.7 101.4 %all-to-all-start.5 = ((bf16[16,16,3,4096]{3,0,2,1:T(8,128)(2,1)}), bf16[16,16,3,4096]{3,0,2,1:T(8,128)(2,1)}, u32[]{:S(2)}, u32[]{:S(2)}) async-start(bf16[16,16,3,4096]{3,0,2,1:T(8,128)(2,1)} %copy.87), calls=%async_computation.5 | async-start | bytes 12582912 | tf_op jit(solution)/shard_map/all_to_all | solution.py:69
where the time goes:
time: 678 us; the launch traced here: 668 us
  waiting for transfers between devices  319 us (47%)
  blocking collectives  149 us (22%)
  local copies, waits for them, and re-layouts  108 us (16%)
  starting transfers between devices  36.2 us (5%)
  matrix products  30.3 us (4%)
  other arithmetic  25.6 us (4%)
    all_to_all x1, blocking collectives, on_device(): lax.all_to_all(terms, 'group', split_axis=0, concat_axis=0, tiled=True)  149 us
    all_to_all x1, waiting for transfers between devices, on_device(): lax.all_to_all(sending, 'group', split_axis=0, concat_axis=0, tiled=True)  137 us
    all_to_all x1, waiting for transfers between devices, on_device(): lax.all_to_all(lax.all_to_all(sending, 'group', split_axis=0, concat_axis...  91 us
    all_to_all x1, waiting for transfers between devices, on_device(): lax.all_to_all(lax.all_to_all(terms, 'group', split_axis=0, concat_axis=0...  90.6 us
    gather x2, local copies, waits for them, and re-layouts, on_device(): tokens[source]  26 us
    reshape x2, local copies, waits for them, and re-layouts, weighted_terms(): return scaled.astype(jnp.bfloat16).reshape(shape_in)  21.7 us
    dot_general x1, matrix products, on_device(): jnp.einsum('tgk,gkd->gtd', selector, returned, preferred_element_type=jnp...  14.9 us
    reshape x1, local copies, waits for them, and re-layouts, weighted_terms(): flat_rows = gathered.reshape(-1, shape_in[-1])  13.7 us
  transfers between devices with their start and end apart: 5, of which 3 were waited for; matrix products, arithmetic and copies ran while one was open for 10% of the time, Pallas kernels for 0%

commit v1 on v0

v1 whole, which is shorter than its diff:
```python
import functools

import jax
import jax.numpy as jnp
from jax import lax
from jax.experimental import pallas as pl
from jax.experimental.pallas import tpu as pltpu
from jax.sharding import PartitionSpec as P

MESH = pl.DeviceIdType.MESH
F32 = jnp.float32
BF16 = jnp.bfloat16

SETS = 4
ROWS = 16
SLOTS = 3
ORDERS = ((0, 1, 2, 3), (1, 0, 3, 2), (2, 3, 0, 1), (3, 2, 1, 0))


def dot(a, b):
    return jnp.dot(a, b, preferred_element_type=F32)


def dot_nt(a, b):
    return lax.dot_general(a, b, (((1,), (1,)), ((), ())), preferred_element_type=F32)


def iota(shape, dim):
    return lax.broadcasted_iota(jnp.int32, shape, dim)


def flip(value, bits):
    if bits == 1:
        return value + 1 - 2 * lax.rem(value, 2)
    if bits == 2:
        return 3 - value
    if bits == 3:
        return lax.rem(value + 2, 4)
    return value


def moved(local, bits):
    y, x = local // 4, lax.rem(local, 4)
    return flip(y, bits & 3) * 4 + flip(x, bits >> 2)


def kernel(
    groups,
    ids_ref, gates_ref, tok_ref, gate_hbm, up_hbm, down_hbm,
    out_ref,
    w_in, w_down, zs, zr, r1, p1, g3, s2, f1, acc, hid,
    take, give, meta_s, meta_r, meta_p, codes, sel, weigh, sel_tmp,
    w_sem, zm_send, zm_recv, pm_send, pm_recv,
    zd_send, zd_recv, zc_send, zc_recv,
    xd_send, xd_recv, xc_send, xc_recv,
):
    tokens = tok_ref.shape[0]
    width = hid.shape[1]
    cols = zs.shape[3]
    held = groups * ROWS
    pad = groups * SLOTS
    segments = groups * 16
    g = lax.axis_index("group")
    l = lax.axis_index("local")

    def rows_of(index):
        return pl.ds(pl.multiple_of(index * ROWS, ROWS), ROWS)

    def peer(j):
        return lax.rem(g + j, groups)

    barrier = pltpu.get_barrier_semaphore()

    def greet(j, carry):
        pl.semaphore_signal(barrier, inc=1, device_id=(peer(j), l), device_id_type=MESH)
        return carry

    lax.fori_loop(1, groups, greet, 0)
    for e in range(4):
        pl.semaphore_signal(barrier, inc=1, device_id=(g, moved(l, 1 << e)), device_id_type=MESH)

    weights = [
        pltpu.make_async_copy(gate_hbm.at[0], w_in.at[:, 0:width], w_sem.at[0]),
        pltpu.make_async_copy(up_hbm.at[0], w_in.at[:, width : 2 * width], w_sem.at[1]),
        pltpu.make_async_copy(down_hbm.at[0], w_down, w_sem.at[2]),
    ]
    for copy in weights:
        copy.start()

    ids = ids_ref[...]
    gates = gates_ref[...].astype(F32)
    label = iota((tokens, segments), 1)
    seg_gate = jnp.zeros((tokens, segments), F32)
    for k in range(ids.shape[1]):
        seg_gate += jnp.where(ids[:, k : k + 1] == label, gates[:, k : k + 1], 0.0)
    is_named = seg_gate > 0
    named = jnp.where(is_named, 1.0, 0.0).astype(BF16)
    in_group = jnp.where(iota((segments, 128), 0) // 16 == iota((segments, 128), 1), 1.0, 0.0).astype(BF16)
    in_group_t = jnp.where(iota((128, segments), 0) == iota((128, segments), 1) // 16, 1.0, 0.0).astype(BF16)
    square = (tokens, tokens)
    below = jnp.where(iota(square, 1) < iota(square, 0), 1.0, 0.0).astype(BF16)
    above = jnp.where(iota(square, 0) < iota(square, 1), 1.0, 0.0).astype(BF16)
    visit = dot(named, in_group) > 0
    place = jnp.where(visit, dot(below, jnp.where(visit, 1.0, 0.0).astype(BF16)), -1.0)
    give[...] = jnp.where(
        dot(place.astype(BF16), in_group_t) == (iota((tokens, held), 1) % ROWS).astype(F32), 1.0, 0.0
    ).astype(BF16)
    visit_t = dot_nt(in_group_t, named) > 0
    place_t = jnp.where(visit_t, dot(jnp.where(visit_t, 1.0, 0.0).astype(BF16), above), -1.0)
    take[...] = jnp.where(
        dot(in_group, place_t.astype(BF16)) == (iota((held, tokens), 0) % ROWS).astype(F32), 1.0, 0.0
    ).astype(BF16)
    rank = jnp.where(is_named, dot(below, named) + 1.0, 0.0).astype(BF16)
    own_group = iota((held, segments), 0) // ROWS == iota((held, segments), 1) // 16
    fold = jnp.where(iota((segments, 128), 0) % 16 == iota((segments, 128), 1), 1.0, 0.0).astype(BF16)
    fold_far = jnp.where(iota((segments, 128), 0) % 16 + 16 == iota((segments, 128), 1), 1.0, 0.0).astype(BF16)
    ranks = jnp.where(own_group, dot(take[...], rank), 0.0).astype(BF16)
    row_gates = jnp.where(own_group, dot(take[...], seg_gate.astype(BF16)), 0.0).astype(BF16)
    meta_s[...] = (dot(ranks, fold) + dot(row_gates, fold_far)).astype(BF16)

    def gather(k):
        for v in range(4):
            part = tok_ref[:, (4 * k + v) * cols : (4 * k + v + 1) * cols]
            zs[k, v] = dot(take[...], part).astype(BF16)

    gather(0)
    pl.semaphore_wait(barrier, groups - 1 + 4)

    def meta_copy(j):
        return pltpu.make_async_remote_copy(
            src_ref=meta_s.at[rows_of(peer(j))], dst_ref=meta_r.at[rows_of(g)],
            send_sem=zm_send.at[j], recv_sem=zm_recv.at[j],
            device_id=(peer(j), l), device_id_type=MESH,
        )

    def out_copy(k, j):
        return pltpu.make_async_remote_copy(
            src_ref=zs.at[k, :, rows_of(peer(j)), :], dst_ref=zr.at[k, :, rows_of(g), :],
            send_sem=zd_send.at[k, j], recv_sem=zd_recv.at[k, j],
            device_id=(peer(j), l), device_id_type=MESH,
        )

    def back_copy(k, j):
        return pltpu.make_async_remote_copy(
            src_ref=zr.at[k, :, rows_of(peer(j)), :], dst_ref=zs.at[k, :, rows_of(g), :],
            send_sem=zc_send.at[k, j], recv_sem=zc_recv.at[k, j],
            device_id=(peer(j), l), device_id_type=MESH,
        )

    def start_all(make):
        def body(j, carry):
            make(j).start()
            return carry

        lax.fori_loop(1, groups, body, 0)

    def wait_all(make):
        def body(j, carry):
            make(j).wait()
            return carry

        lax.fori_loop(1, groups, body, 0)

    def start_out(k):
        start_all(functools.partial(out_copy, k))

    def exchange(e, src, dst, send, recv):
        return pltpu.make_async_remote_copy(
            src_ref=src, dst_ref=dst, send_sem=send, recv_sem=recv,
            device_id=(g, moved(l, 1 << e)), device_id_type=MESH,
        )

    def forth(k, v, step):
        kv = k * 4 + v
        src, dst = (
            (zr.at[k, v], r1.at[kv]),
            (s2.at[kv], g3.at[kv, 0:2, :, 1]),
            (g3.at[kv, 0], g3.at[kv, 2]),
            (g3.at[kv, 1:3, 1], f1.at[kv]),
        )[step]
        return exchange(ORDERS[v][step], src, dst, xd_send.at[step, kv], xd_recv.at[step, kv])

    def back(k, v, step):
        kv = k * 4 + v
        src, dst = (
            (r1.at[kv], p1.at[kv]),
            (g3.at[kv, 0:2, :, 1], s2.at[kv]),
            (g3.at[kv, 2], g3.at[kv, 0]),
            (f1.at[kv], g3.at[kv, 1:3, 1]),
        )[step]
        return exchange(ORDERS[v][step], src, dst, xc_send.at[step, kv], xc_recv.at[step, kv])

    def partner_meta(e):
        return exchange(e, meta_r, meta_p.at[e], pm_send.at[e], pm_recv.at[e])

    start_all(meta_copy)
    start_out(0)
    gather(1)
    start_out(1)
    for k in range(2, SETS):
        gather(k)
    meta_r[rows_of(g), :] = meta_s[rows_of(g), :]
    wait_all(meta_copy)
    for e in range(4):
        partner_meta(e).start()

    eye = jnp.where(iota((128, 128), 0) == iota((128, 128), 1), 1.0, 0.0).astype(BF16)
    eye_held = jnp.where(iota((held, held), 0) == iota((held, held), 1), 1.0, 0.0).astype(BF16)
    base = (iota((16, held), 1) // ROWS * SLOTS - 1).astype(F32)
    slot = iota((pad, held), 0).astype(F32)

    def decode(index, meta):
        turned = dot_nt(eye, meta)
        codes[index, 0:16] = jnp.where(turned[0:16] > 0, base + turned[0:16], -1.0)
        codes[index, 16:32] = turned[16:32]

    def build(v, r):
        e1, e2, e3, e4 = ORDERS[v]
        index = 1 + e1 if r else 0
        for d2 in range(2):
            for q in range(2):
                for d4 in range(2):
                    place = moved(l, d2 << e2 | (1 - q) << e3 | d4 << e4)
                    b = (d2 * 2 + q) * 2 + d4
                    hit = slot == codes[index, pl.ds(place, 1), :]
                    sel[v, r, b * pad : (b + 1) * pad, :] = jnp.where(hit, 1.0, 0.0).astype(BF16)
                    sel_tmp[b * pad : (b + 1) * pad, :] = jnp.where(
                        hit, codes[index, pl.ds(place + 16, 1), :], 0.0
                    ).astype(BF16)
        weigh[v, r] = dot_nt(eye_held, sel_tmp[...]).astype(BF16)

    decode(0, meta_r[...])
    for v in range(4):
        build(v, 0)
    for e in range(4):
        partner_meta(e).wait()
        decode(1 + e, meta_p[e])
    for v in range(4):
        build(v, 1)

    acc[...] = jnp.zeros_like(acc)
    for copy in weights:
        copy.wait()

    def select(k, v, r, rows):
        kv = k * 4 + v
        chosen = dot(sel[v, r], rows).astype(BF16)
        for q in range(2):
            for d4 in range(2):
                b = q * 2 + d4
                g3[kv, q, d4, 0, r * pad : (r + 1) * pad, :] = chosen[b * pad : (b + 1) * pad]
                b += 4
                s2[kv, q, d4, r * pad : (r + 1) * pad, :] = chosen[b * pad : (b + 1) * pad]

    def block_of(v, r4, r3, r2, r1_):
        e1, e2, e3, e4 = ORDERS[v]
        return r4 << e4 | r3 << e3 | r2 << e2 | r1_ << e1

    def accumulate(k, v, r4, rows):
        at = pl.ds(pl.multiple_of((k * 4 + v) * cols, cols), cols)
        part = dot(rows.reshape(8 * pad, cols), w_in[at, :])
        for b in range(8):
            c = block_of(v, r4, b >> 2, b >> 1 & 1, b & 1)
            acc[c] += part[b * pad : (b + 1) * pad]

    def forth_a(k):
        for v in range(4):
            zr[k, v, rows_of(g), :] = zs[k, v, rows_of(g), :]
        wait_all(functools.partial(out_copy, k))
        for v in range(4):
            forth(k, v, 0).start()

        @pl.when(k + 2 < SETS)
        def _():
            start_out(k + 2)

        for v in range(4):
            select(k, v, 0, zr[k, v])

    def forth_b(k):
        for v in range(4):
            forth(k, v, 0).wait()
            select(k, v, 1, r1[k * 4 + v])
            forth(k, v, 1).start()

    def forth_c(k):
        for v in range(4):
            forth(k, v, 1).wait()
            forth(k, v, 2).start()

    def forth_d(k):
        for v in range(4):
            forth(k, v, 2).wait()
            forth(k, v, 3).start()
        for v in range(4):
            accumulate(k, v, 0, g3[k * 4 + v, 1:3, 0])

    def forth_e(k):
        for v in range(4):
            forth(k, v, 3).wait()
            accumulate(k, v, 1, f1[k * 4 + v])

    def pipeline(stages):
        depth = len(stages)

        def body(t, carry):
            for lag in range(depth - 1, -1, -1):
                k = t - lag

                @pl.when((k >= 0) & (k < SETS))
                def _(stage=stages[lag], k=k):
                    stage(k)

            return carry

        lax.fori_loop(0, SETS + depth - 1, body, 0)

    pipeline((forth_a, forth_b, forth_c, forth_d, forth_e))

    for c in range(16):
        gated = acc[c, :, 0:width]
        upward = acc[c, :, width : 2 * width]
        hid[c * pad : (c + 1) * pad, :] = (gated / (1.0 + jnp.exp(-gated)) * upward).astype(BF16)

    def back_a(k):
        for v in range(4):
            kv = k * 4 + v
            at = pl.ds(pl.multiple_of(kv * cols, cols), cols)
            result = dot(hid[...], w_down[:, at]).astype(BF16)
            for b in range(8):
                r3, r2, r1_ = b >> 2, b >> 1 & 1, b & 1
                inner = slice(r1_ * pad, (r1_ + 1) * pad)
                c = block_of(v, 1, r3, r2, r1_)
                f1[kv, r3, r2, inner, :] = result[c * pad : (c + 1) * pad]
                c = block_of(v, 0, r3, r2, r1_)
                g3[kv, 1 + r3, 0, r2, inner, :] = result[c * pad : (c + 1) * pad]
            back(k, v, 3).start()

    def back_b(k):
        for v in range(4):
            back(k, v, 3).wait()
            back(k, v, 2).start()

    def back_c(k):
        for v in range(4):
            back(k, v, 2).wait()
            back(k, v, 1).start()

    def part_sum(k, v, r):
        kv = k * 4 + v
        inner = slice(r * pad, (r + 1) * pad)
        near = g3[kv, 0:2, :, 0, inner, :].reshape(4 * pad, cols)
        far = s2[kv, :, :, inner, :].reshape(4 * pad, cols)
        return dot(weigh[v, r], jnp.concatenate([near, far], axis=0))

    def back_d(k):
        for v in range(4):
            back(k, v, 1).wait()
            r1[k * 4 + v] = part_sum(k, v, 1).astype(BF16)
            back(k, v, 0).start()

    def back_e(k):
        for v in range(4):
            own = part_sum(k, v, 0)
            back(k, v, 0).wait()
            zr[k, v] = (own + p1[k * 4 + v].astype(F32)).astype(BF16)
        start_all(functools.partial(back_copy, k))
        for v in range(4):
            zs[k, v, rows_of(g), :] = zr[k, v, rows_of(g), :]

    def back_f(k):
        wait_all(functools.partial(back_copy, k))
        for v in range(4):
            at = pl.ds(pl.multiple_of((k * 4 + v) * cols, cols), cols)
            out_ref[:, at] = dot(give[...], zs[k, v]).astype(BF16)

    pipeline((back_a, back_b, back_c, back_d, back_e, back_f))


def on_device(tokens, segment_ids, segment_count, gate_values, gate_weight, up_weight, down_weight):
    groups = lax.axis_size("group")
    model = tokens.shape[1]
    width = gate_weight.shape[2]
    cols = model // (4 * SETS)
    held = groups * ROWS
    pad = groups * SLOTS
    is_valid = lax.broadcasted_iota(jnp.int32, segment_ids.shape, 1) < segment_count[:, None]
    ids = jnp.where(is_valid, segment_ids, -1)
    vmem = pl.BlockSpec(memory_space=pltpu.VMEM)
    hbm = pl.BlockSpec(memory_space=pl.ANY)
    dma = pltpu.SemaphoreType.DMA
    return pl.pallas_call(
        functools.partial(kernel, groups),
        out_shape=jax.ShapeDtypeStruct(tokens.shape, BF16),
        in_specs=[vmem, vmem, vmem, hbm, hbm, hbm],
        out_specs=vmem,
        scratch_shapes=[
            pltpu.VMEM((model, 2 * width), BF16),
            pltpu.VMEM((width, model), BF16),
            pltpu.VMEM((SETS, 4, held, cols), BF16),
            pltpu.VMEM((SETS, 4, held, cols), BF16),
            pltpu.VMEM((SETS * 4, held, cols), BF16),
            pltpu.VMEM((SETS * 4, held, cols), BF16),
            pltpu.VMEM((SETS * 4, 3, 2, 2, 2 * pad, cols), BF16),
            pltpu.VMEM((SETS * 4, 2, 2, 2 * pad, cols), BF16),
            pltpu.VMEM((SETS * 4, 2, 2, 2 * pad, cols), BF16),
            pltpu.VMEM((16, pad, 2 * width), F32),
            pltpu.VMEM((16 * pad, width), BF16),
            pltpu.VMEM((held, tokens.shape[0]), BF16),
            pltpu.VMEM((tokens.shape[0], held), BF16),
            pltpu.VMEM((held, 128), BF16),
            pltpu.VMEM((held, 128), BF16),
            pltpu.VMEM((4, held, 128), BF16),
            pltpu.VMEM((5, 32, held), F32),
            pltpu.VMEM((4, 2, 8 * pad, held), BF16),
            pltpu.VMEM((4, 2, held, 8 * pad), BF16),
            pltpu.VMEM((8 * pad, held), BF16),
            dma((3,)),
            dma((groups,)), dma((groups,)), dma((4,)), dma((4,)),
            dma((SETS, groups)), dma((SETS, groups)), dma((SETS, groups)), dma((SETS, groups)),
            dma((4, SETS * 4)), dma((4, SETS * 4)), dma((4, SETS * 4)), dma((4, SETS * 4)),
        ],
        compiler_params=pltpu.CompilerParams(
            collective_id=0, has_side_effects=True, vmem_limit_bytes=56 * 1024 * 1024
        ),
    )(ids, gate_values, tokens, gate_weight, up_weight, down_weight)


def solution(mesh):
    return jax.shard_map(
        on_device,
        mesh=mesh,
        in_specs=(
            P(("group", "local"), None),
            P(("group", "local"), None),
            P(("group", "local")),
            P(("group", "local"), None),
            P(("group", "local"), None, None),
            P(("group", "local"), None, None),
            P(("group", "local"), None, None),
        ),
        out_specs=P(("group", "local"), None),
        check_vma=False,
    )
```

time: 678 us -> 205 us (0.30); the launches traced: 668 us -> 204 us
  waiting for transfers between devices: 319 us -> 0 us
  Pallas kernels: 0 us -> 199 us
  blocking collectives: 149 us -> 0 us
  local copies, waits for them, and re-layouts: 108 us -> 4.03 us
  starting transfers between devices: 36.2 us -> 0 us
  matrix products: 30.3 us -> 0 us
  other arithmetic: 25.6 us -> 1.34 us
    all_to_all x5 -> x0, waiting for transfers between devices: 319 us -> none  [the longest x1 137 us: on_device(): lax.all_to_all(sending, 'group', split_axis=0, concat_axis=0, tiled=True)]
    pallas_call x0 -> x1, Pallas kernels: none -> 199 us  [on_device(): pl.pallas_call(functools.partial(kernel, groups), out_shape=jax.ShapeDtyp...]
    all_to_all x1 -> x0, blocking collectives: 149 us -> none  [on_device(): lax.all_to_all(terms, 'group', split_axis=0, concat_axis=0, tiled=True)]
    all_to_all x5 -> x0, starting transfers between devices: 36.2 us -> none  [the longest x1 9.98 us: on_device(): lax.all_to_all(slot_gate, 'group', split_axis=0, concat_axis=0, tiled=True)]
    reshape x3 -> x0, local copies, waits for them, and re-layouts: 35.5 us -> none  [the longest x2 21.7 us: weighted_terms(): return scaled.astype(jnp.bfloat16).reshape(shape_in)]
    all_to_all x5 -> x0, local copies, waits for them, and re-layouts: 30.6 us -> none  [the longest x1 11.4 us: on_device(): lax.all_to_all(lax.all_to_all(sending, 'group', split_axis=0, concat_axis...]
    dot_general x4 -> x0, matrix products: 30.3 us -> none  [the longest x1 14.9 us: on_device(): jnp.einsum('tgk,gkd->gtd', selector, returned, preferred_element_type=jnp...]
    gather x2 -> x0, local copies, waits for them, and re-layouts: 26 us -> none  [on_device(): tokens[source]]
  transfers between devices with their start and end apart: 5 -> 0, of which waited for: 3 -> 0; matrix products, arithmetic and copies ran while one was open for 10% -> 0% of each run, Pallas kernels for 0% -> 0%
where the time goes in v1:
time: 205 us; the launch traced here: 204 us
  Pallas kernels  199 us (97%)
  local copies, waits for them, and re-layouts  4.03 us (2%)
    pallas_call x1, Pallas kernels, on_device(): pl.pallas_call(functools.partial(kernel, groups), out_shape=jax.ShapeDtyp...  199 us

profile of v1, /device:TPU:1, one launch (start us, length us, event | category | flops | bytes accessed | tf_op | source)
XLA Modules:
  0.0 204.3 jit_solution(7900308862444733807)
XLA Ops:
  0.0 1.4 copy.9.gates_ref
  1.4 0.8 copy.8
  2.2 1.3 fusion.ids_ref
  3.5 198.9 %shard_map.73 = bf16[64,4096]{1,0:T(8,128)(2,1)} custom-call(s32[64,12]{1,0:T(8,128)} %fusion.ids_ref, bf16[64,12]{1,0:T(8,128)(2,1)} %copy.9.gates_ref, bf16[64,4096]{1,0:T(8,128)(2,1)} %tok_ref.1, bf16[1,4096,384]{2,1,0:T(8,128)(2,1)} %gate_hbm.1, bf16[1,4096,384]{2,1,0:T(8,128)(2,1)} %up_hbm.1, bf16[1,384,4096]{2,1,0:T(8,128)(2,1)} %down_hbm.1), custom_call_target="tpu_custom_call" | custom-call | tf_op jit(solution)/shard_map/pallas_call | solution.py:392
  202.5 1.9 copy.11
